TPU v7x, 256 devices: a whole 4x4x8 slice. The times are simulated.
256 devices in a mesh: cfg: 2 (over core), seq: 16 (over x, z_hi), dp: 8 (over y, z_lo).
Axes of the slice: x: 4, y: 4, z: 8 (z_hi: 4, z_lo: 2; z = z_hi * 2 + z_lo), core: 2. Of those that a mesh axis runs over, the one named last changes fastest.
Arguments:
- image_projections: bfloat16 [2, 16, 2048, 6144], P('cfg', 'dp', 'seq'), may hold values from -8 to 8
- text_projections: bfloat16 [2, 16, 512, 4096], P('cfg', 'dp', 'seq'), may hold values from -6 to 6
- output_weight: bfloat16 [2048, 3072], P('seq', 'dp'), may hold values from -0.125 to 0.125
- image_state: bfloat16 [2, 16, 2048, 3072], P('cfg', 'dp', 'seq'), may hold values from -6 to 6
- modulation: bfloat16 [2, 16, 3, 3072], P('cfg', 'dp'), may hold values from -4 to 4
- final_weight: bfloat16 [3072, 64], replicated, may hold values from -0.109375 to 0.109375
- latent: float32 [16, 2048, 64], P('dp', 'seq'), may hold values from -6 to 6
- next_latent: float32 [16, 2048, 64], P('dp', 'seq'), may hold values from -8 to 8
- timestep: float32 [16], P('dp'), may hold values from 0.3 to 0.8
- rewards: float32 [16], P('dp'), may hold values from -5 to 5
- group_index: int32 [16], P('dp'), may hold values from 0 to 7, as said below
Outputs:
- grad_final_weight: float32 [3072, 64], P('dp')
- log_prob: float32 [16], P('dp')
Inputs may be any that keep to these rules, and one draw needn't show every extreme that they name: `group_index`: each of the 8 prompts has exactly 2 rollouts; rollout 0 shares its prompt with one of the last 2 rollouts.
All inputs are finite; a program needn't handle non-finite values.
Results may differ from a plain program's by a relative error of at most 0.00053.
Values may be sent and summed in bfloat16 or wider, within the bound.
No kernel may reach another device: no remote copies, remote signals or barrier semaphores. Data moves between devices by JAX's collectives and lax.ppermute only.
A program may use at most 64 MiB of HBM per device.

v0:
```python
import functools
import math

import jax
import jax.numpy as jnp
from jax import lax
from jax.experimental import pallas as pl
from jax.experimental.pallas import tpu as pltpu
from jax.sharding import PartitionSpec as P

C = 64
HD = 128
GROUP_SIZE = 2

cfg_scale = 4.5
noise_level = 0.7
step_width = 0.02
norm_eps = 1e-06

X, ZH, Y, ZL = 4, 4, 4, 2
VMEM_BYTES = 32 * 1024 * 1024
HIDDEN_VMEM_BYTES = 40 * 1024 * 1024
FULL_VMEM_BYTES = 61 * 1024 * 1024


def from_x(value, d):
    pairs = [(((x + d) % X) * ZH + z, x * ZH + z) for x in range(X) for z in range(ZH)]
    return lax.ppermute(value, "seq", pairs)


def from_column(value, d):
    def at(core, x, z, y, zl):
        return ((core * X + x) * ZH + z) * (Y * ZL) + y * ZL + zl

    pairs = [
        (at(core if zl == core else 1 - core, x, (z + d) % ZH, y, core), at(core, x, z, y, zl))
        for core in range(2)
        for x in range(X)
        for z in range(ZH)
        for y in range(Y)
        for zl in range(ZL)
    ]
    return lax.ppermute(value, ("cfg", "seq", "dp"), pairs)


def from_zh(value, d):
    pairs = [(x * ZH + (z + d) % ZH, x * ZH + z) for x in range(X) for z in range(ZH)]
    return lax.ppermute(value, "seq", pairs)


def from_y(value, d):
    pairs = [(((y + d) % Y) * ZL + z, y * ZL + z) for y in range(Y) for z in range(ZL)]
    return lax.ppermute(value, "dp", pairs)


def from_zl(value):
    pairs = [(y * ZL + 1 - z, y * ZL + z) for y in range(Y) for z in range(ZL)]
    return lax.ppermute(value, "dp", pairs)


def from_cfg(value):
    return lax.ppermute(value, "cfg", [(0, 1), (1, 0)])


def after(value, *others):
    return lax.optimization_barrier((value,) + others)[0]


def ring_sum(value, fetch):
    first, second, third = (fetch(value, d) for d in (1, 2, 3))
    return (value + second) + (first + third)


def pack_kernel(k_ref, v_ref, kt_ref, vt_ref, q_ref, out_ref):
    rows, text = k_ref.shape[2], kt_ref.shape[2]
    for h in range(out_ref.shape[0]):
        cols = slice(h * HD, (h + 1) * HD)
        at = 0
        for r in range(k_ref.shape[1]):
            for ref, count in ((k_ref, rows), (kt_ref, text), (v_ref, rows), (vt_ref, text)):
                out_ref[h, at : at + count, :] = ref[0, r, :, cols]
                at += count
        out_ref[h, at : at + rows, :] = q_ref[0, 0, :, cols]


def pack_queries_kernel(q_ref, out_ref):
    for h in range(out_ref.shape[0]):
        out_ref[h] = q_ref[0, 0, :, h * HD : (h + 1) * HD]


def pack(image_projections, text_projections):
    _, per_dev, rows, width = image_projections.shape
    text = text_projections.shape[2]
    heads = width // (3 * HD)
    per = 4
    steps = heads // per
    total = per_dev * 2 * (rows + text) + rows

    def spec(rollouts, count, part):
        return pl.BlockSpec((1, rollouts, count, per * HD), lambda h: (0, 0, 0, part * steps + h))

    return pl.pallas_call(
        pack_kernel,
        grid=(steps,),
        in_specs=[
            spec(per_dev, rows, 1),
            spec(per_dev, rows, 2),
            spec(per_dev, text, 0),
            spec(per_dev, text, 1),
            spec(1, rows, 0),
        ],
        out_specs=pl.BlockSpec((per, total, HD), lambda h: (h, 0, 0)),
        out_shape=jax.ShapeDtypeStruct((heads, total, HD), jnp.bfloat16),
        compiler_params=pltpu.CompilerParams(vmem_limit_bytes=FULL_VMEM_BYTES),
        cost_estimate=pl.CostEstimate(
            flops=0, bytes_accessed=2 * heads * total * HD * 2, transcendentals=0
        ),
        name="pack",
    )(image_projections, image_projections, text_projections, text_projections, image_projections)


def pack_queries(image_projections, r):
    _, _, rows, width = image_projections.shape
    heads = width // (3 * HD)
    return pl.pallas_call(
        pack_queries_kernel,
        grid=(1,),
        in_specs=[pl.BlockSpec((1, 1, rows, heads * HD), lambda i: (0, r, 0, 0))],
        out_specs=pl.BlockSpec((heads, rows, HD), lambda i: (0, 0, 0)),
        out_shape=jax.ShapeDtypeStruct((heads, rows, HD), jnp.bfloat16),
        compiler_params=pltpu.CompilerParams(vmem_limit_bytes=VMEM_BYTES),
        cost_estimate=pl.CostEstimate(
            flops=0, bytes_accessed=2 * heads * rows * HD * 2, transcendentals=0
        ),
        name="pack_queries",
    )(image_projections)


def attention_kernel(q_ref, kv_ref, *rest):
    out_ref, keys, values = rest[-3:]
    peers, kv_rows = kv_ref.shape[0], kv_ref.shape[1] // 2
    ones = jnp.ones((kv_rows, HD), jnp.bfloat16)
    for s in range(peers):
        at = slice(s * kv_rows, (s + 1) * kv_rows)
        keys[at, :] = kv_ref[s, 0:kv_rows, :]
        values[at, 0:HD] = kv_ref[s, kv_rows : 2 * kv_rows, :]
        values[at, HD : 2 * HD] = ones

    factor = math.log2(math.e) / math.sqrt(HD)
    for n in range(peers):
        scores = lax.dot_general(
            q_ref[n], keys[...], (((1,), (1,)), ((), ())), preferred_element_type=jnp.float32
        )
        highest = jnp.max(scores, axis=1, keepdims=True)
        powered = jnp.exp2((scores - highest) * factor).astype(jnp.bfloat16)
        sums = jnp.dot(powered, values[...], preferred_element_type=jnp.float32)
        out_ref[n] = (sums[:, 0:HD] / sums[:, HD : HD + 1]).astype(jnp.bfloat16)


def attention(queries, q_at, key_values, r, rows, kv_rows, per_dev, earlier=()):
    peers = queries.shape[0]
    return pl.pallas_call(
        attention_kernel,
        grid=(1,),
        in_specs=[
            pl.BlockSpec((peers, rows, HD), lambda i: (0, q_at, 0)),
            pl.BlockSpec((peers, 2 * kv_rows, HD), lambda i: (0, r, 0)),
        ]
        + [pl.BlockSpec(memory_space=pl.ANY)] * len(earlier),
        out_specs=pl.BlockSpec((peers, rows, HD), lambda i: (0, r, 0)),
        out_shape=jax.ShapeDtypeStruct((peers, per_dev * rows, HD), jnp.bfloat16),
        scratch_shapes=[
            pltpu.VMEM((peers * kv_rows, HD), jnp.bfloat16),
            pltpu.VMEM((peers * kv_rows, 2 * HD), jnp.bfloat16),
        ],
        input_output_aliases={2: 0} if earlier else {},
        compiler_params=pltpu.CompilerParams(vmem_limit_bytes=FULL_VMEM_BYTES),
        cost_estimate=pl.CostEstimate(
            flops=8 * peers * rows * peers * kv_rows * HD,
            bytes_accessed=2 * peers * (2 * rows + 2 * kv_rows) * HD,
            transcendentals=peers * rows * peers * kv_rows,
        ),
        name=f"attention{r}",
    )(queries, key_values, *earlier)


def hidden_kernel(place, heads_ref, state_ref, mods_ref, final_ref, *rest):
    pieces, (hidden_ref, velocity_ref, flat, mixed, weights, sems) = rest[:10], rest[10:]
    x_at, zh_at, y_at, c_at = place[0], place[1], place[2], place[3]
    per_dev, rows = state_ref.shape[1], state_ref.shape[2]
    width = weights.shape[2]
    depth = weights.shape[1]
    spans = ((0, 0), (1, 0), (3, 0), (2, 0), (2, depth // 2))
    copies = []
    for core in range(2):
        for n, (turn, at_row) in enumerate(spans):
            piece = pieces[core * 5 + n]
            copy = pltpu.make_async_copy(
                piece,
                weights.at[core * 4 + turn, pl.ds(at_row, piece.shape[0])],
                sems.at[core * 5 + n],
            )
            copy.start()
            copies.append(copy)
    for i in range(X):
        for j in range(ZH):
            head = lax.rem(x_at + i, X) * ZH + lax.rem(zh_at + j, ZH)
            k = i * ZH + j
            flat[:, k * HD : (k + 1) * HD] = heads_ref[head]
    row_sum = jnp.zeros((per_dev * rows, 1), jnp.float32)
    square_sum = jnp.zeros((per_dev * rows, 1), jnp.float32)
    for core in range(2):
        core_at = c_at if core == 0 else 1 - c_at
        for turn, needed in ((0, (0,)), (1, (1,)), (3, (2,)), (2, (3, 4))):
            for n in needed:
                copies[core * 5 + n].wait()
            at = pl.ds(pl.multiple_of((lax.rem(y_at + turn, Y) * ZL + core_at) * width, 128), width)
            projected = jnp.dot(
                flat[...], weights[core * 4 + turn], preferred_element_type=jnp.float32
            )
            for r in range(per_dev):
                gate = mods_ref[0, r : r + 1, at].astype(jnp.float32)
                mixed[r * rows : (r + 1) * rows, at] = (
                    state_ref[0, r, :, at].astype(jnp.float32)
                    + gate * projected[r * rows : (r + 1) * rows]
                )
            block = mixed[:, at]
            row_sum = row_sum + jnp.sum(block, axis=1, keepdims=True)
            square_sum = square_sum + jnp.sum(block * block, axis=1, keepdims=True)
    width_all = mixed.shape[1]
    center = row_sum / width_all
    square = square_sum / width_all
    inverse = lax.rsqrt(square - center * center + norm_eps)
    for r in range(per_dev):
        at = slice(r * rows, (r + 1) * rows)
        scale = 1.0 + mods_ref[2, r : r + 1, :].astype(jnp.float32)
        shift = mods_ref[1, r : r + 1, :].astype(jnp.float32)
        hidden_ref[at, :] = (
            (mixed[at, :] - center[at]) * inverse[at] * scale + shift
        ).astype(jnp.bfloat16)
    velocity_ref[...] = lax.dot_general(
        final_ref[...], hidden_ref[...], (((1,), (1,)), ((), ())), preferred_element_type=jnp.float32
    )


def hidden_rows(place, heads_part, image_state, modulation, final_weight, pieces):
    heads, all_rows, _ = heads_part.shape
    width_all = image_state.shape[3]
    vmem = pl.BlockSpec(memory_space=pltpu.VMEM)
    return pl.pallas_call(
        hidden_kernel,
        in_specs=[pl.BlockSpec(memory_space=pltpu.SMEM)]
        + [vmem] * 4
        + [pl.BlockSpec(memory_space=pl.ANY)] * 10,
        out_specs=[vmem] * 2,
        out_shape=[
            jax.ShapeDtypeStruct((all_rows, width_all), jnp.bfloat16),
            jax.ShapeDtypeStruct((C, all_rows), jnp.float32),
        ],
        scratch_shapes=[
            pltpu.VMEM((all_rows, heads * HD), jnp.bfloat16),
            pltpu.VMEM((all_rows, width_all), jnp.float32),
            pltpu.VMEM((8, heads * HD, pieces[0].shape[1]), jnp.bfloat16),
            pltpu.SemaphoreType.DMA((10,)),
        ],
        compiler_params=pltpu.CompilerParams(vmem_limit_bytes=HIDDEN_VMEM_BYTES),
        cost_estimate=pl.CostEstimate(
            flops=2 * all_rows * heads * HD * width_all,
            bytes_accessed=2 * heads * HD * width_all,
            transcendentals=0,
        ),
        name="hidden",
    )(place, heads_part, image_state, modulation, final_weight, *pieces)


def step_kernel(
    place, terms, own_ref, partner_ref, latent_ref, next_ref, hidden_ref, keep_ref, send_ref, squares_ref
):
    first = place[3] == 0
    own, partner = own_ref[...], partner_ref[...]
    conditional = jnp.where(first, own, partner)
    unconditional = jnp.where(first, partner, own)
    guided = unconditional + cfg_scale * (conditional - unconditional)
    per_dev, _, rows = latent_ref.shape
    row = lax.broadcasted_iota(jnp.int32, squares_ref.shape, 0)
    squares = jnp.zeros(squares_ref.shape, jnp.float32)
    slopes = []
    for r in range(per_dev):
        step_mean = (
            latent_ref[r] * terms[0, r] - guided[:, r * rows : (r + 1) * rows] * terms[1, r]
        )
        residue = next_ref[r] - step_mean
        squares = jnp.where(row == r, jnp.sum(residue * residue), squares)
        slopes.append(terms[2, r] * residue)
    squares_ref[...] = squares
    own_slopes = jnp.where(first, cfg_scale, 1.0 - cfg_scale) * jnp.concatenate(slopes, axis=1)
    half = own_slopes.shape[0] // 2
    low, high = own_slopes[:half], own_slopes[half:]
    ordered = jnp.concatenate([jnp.where(first, low, high), jnp.where(first, high, low)], axis=0)
    partial = jnp.dot(
        ordered.astype(jnp.bfloat16), hidden_ref[...], preferred_element_type=jnp.float32
    )
    width = keep_ref.shape[2]
    for n in range(keep_ref.shape[0]):
        cols = slice(n * width, (n + 1) * width)
        keep_ref[n] = partial[:half, cols]
        send_ref[n] = partial[half:, cols]


def step(place, terms, own, partner, latent, next_latent, hidden, data_count):
    rows, width_all = hidden.shape
    cut = (data_count, C // 2, width_all // data_count)
    smem = pl.BlockSpec(memory_space=pltpu.SMEM)
    vmem = pl.BlockSpec(memory_space=pltpu.VMEM)
    return pl.pallas_call(
        step_kernel,
        in_specs=[smem] * 2 + [vmem] * 5,
        out_specs=[vmem] * 3,
        out_shape=[
            jax.ShapeDtypeStruct(cut, jnp.float32),
            jax.ShapeDtypeStruct(cut, jnp.float32),
            jax.ShapeDtypeStruct((8, 128), jnp.float32),
        ],
        compiler_params=pltpu.CompilerParams(vmem_limit_bytes=VMEM_BYTES),
        cost_estimate=pl.CostEstimate(
            flops=2 * rows * C * width_all, bytes_accessed=2 * rows * width_all, transcendentals=0
        ),
        name="step",
    )(place, terms, own, partner, latent, next_latent, hidden)


def fold_kernel(parts_ref, squares_ref, out_ref):
    count, width = parts_ref.shape[1], parts_ref.shape[2]
    out_ref[0:count, :] = jnp.sum(parts_ref[...], axis=0)
    out_ref[count : count + 8, 128:width] = jnp.zeros((8, width - 128), jnp.float32)
    out_ref[count : count + 8, 0:128] = squares_ref[...]


def fold(parts, squares):
    _, count, width = parts.shape
    vmem = pl.BlockSpec(memory_space=pltpu.VMEM)
    return pl.pallas_call(
        fold_kernel,
        in_specs=[vmem] * 2,
        out_specs=vmem,
        out_shape=jax.ShapeDtypeStruct((count + 8, width), jnp.float32),
        name="fold",
    )(parts, squares)


def exchange(send):
    return lax.all_to_all(send, "seq", split_axis=0, concat_axis=0, tiled=True)


def per_device(
    image_projections,
    text_projections,
    output_weight,
    image_state,
    modulation,
    final_weight,
    latent,
    next_latent,
    timestep,
    rewards,
    group_index,
):
    seq_count = lax.axis_size("seq")
    data_count = lax.axis_size("dp")
    per_dev = image_projections.shape[1]
    image_count = image_projections.shape[2]
    width_all = image_state.shape[3]
    rollouts = per_dev * data_count
    seq_at, dp_at, c_at = lax.axis_index("seq"), lax.axis_index("dp"), lax.axis_index("cfg")
    x_at, zh_at, y_at = seq_at // ZH, seq_at % ZH, dp_at // ZL
    place = jnp.stack([x_at, zh_at, y_at, c_at]).astype(jnp.int32)

    kv_rows = image_count + text_projections.shape[2]

    group_count = rollouts // GROUP_SIZE
    member = (group_index[:, None] == jnp.arange(group_count, dtype=jnp.int32)[None, :]).astype(
        jnp.float32
    )
    column = jnp.concatenate([from_column(output_weight, d) for d in range(ZH)], axis=0)
    totals = jnp.sum(member * rewards[:, None], axis=0)
    first_part = exchange(after(pack(image_projections, text_projections), column))
    totals = ring_sum(totals, from_y)
    column = after(column, totals)
    totals = totals + from_zl(totals)
    advantage = rewards - jnp.sum(member * totals[None, :], axis=1) / GROUP_SIZE
    plane = jnp.concatenate([column] + [from_x(column, d) for d in range(1, X)], axis=0)
    cut = plane.shape[0] // 2
    ahead, behind = from_y(plane, 1), from_y(plane, -1)
    plane_other = from_cfg(plane)
    second_part = exchange(
        after(pack_queries(image_projections, 1), plane_other, first_part)
    )
    far_first = from_y(ahead[:cut], 1)
    far_second = from_y(behind[cut:], -1)
    own = [plane, ahead, behind, far_first, far_second]
    pieces = own + [plane_other] + [from_cfg(piece) for piece in own[1:]]

    spread = noise_level * jnp.sqrt(timestep / (1.0 - timestep))
    drift_gain = 1.0 + spread * spread * (1.0 - timestep) / (2.0 * timestep)
    deviation = spread * math.sqrt(step_width)
    terms = jnp.stack(
        [
            1.0 - spread * spread / (2.0 * timestep) * step_width,
            drift_gain * step_width,
            advantage / (rollouts * C) * drift_gain * step_width / (deviation * deviation),
        ]
    )

    queries_at = per_dev * 2 * kv_rows // image_count
    attended = attention(first_part, queries_at, first_part, 0, image_count, kv_rows, per_dev)
    attended = attention(
        after(second_part, ahead, behind), 0, first_part, 1, image_count, kv_rows, per_dev, (attended,)
    )
    returned = after(exchange(attended), terms)
    hidden, velocity = hidden_rows(
        place, returned, image_state, modulation[0].transpose(1, 0, 2), final_weight.T, pieces
    )
    keep, send, squares = step(
        place,
        terms,
        velocity,
        from_cfg(velocity),
        latent.transpose(0, 2, 1),
        next_latent.transpose(0, 2, 1),
        hidden,
        data_count,
    )

    kept = keep + from_cfg(send)
    share = fold(lax.all_to_all(kept, "dp", split_axis=0, concat_axis=0, tiled=True), squares)
    share = ring_sum(ring_sum(share, from_zh), from_x)
    other = from_cfg(share)
    first = c_at == 0
    half = C // 2
    gradient = jnp.concatenate(
        [jnp.where(first, share, other)[:half], jnp.where(first, other, share)[:half]], axis=0
    ).T
    square_mean = share[half : half + per_dev, 0] / (seq_count * image_count * C)
    log_prob = (
        -square_mean / (2.0 * deviation * deviation)
        - jnp.log(deviation)
        - 0.5 * math.log(2.0 * math.pi)
    )
    return (gradient, log_prob)


def solution(mesh):
    in_specs = (
        P("cfg", "dp", "seq", None),
        P("cfg", "dp", "seq", None),
        P("seq", "dp"),
        P("cfg", "dp", "seq", None),
        P("cfg", "dp", None, None),
        P(),
        P("dp", "seq", None),
        P("dp", "seq", None),
        P("dp"),
        P("dp"),
        P("dp"),
    )
    out_specs = (P("dp", None), P("dp"))
    return jax.shard_map(
        per_device, mesh=mesh, in_specs=in_specs, out_specs=out_specs, check_vma=False
    )
```

profile of v0, /device:TPU:1, one launch (start us, length us, event | category | flops | bytes accessed | tf_op | source)
XLA Modules:
  0.0 242.0 jit_solution(13701508971632677894)
XLA Ops:
  0.6 4.9 %collective-permute-start.4 = (bf16[128,384]{1,0:T(8,128)(2,1)}, bf16[128,384]{1,0:T(8,128)(2,1)S(1)}, u32[]{:S(2)}, u32[]{:S(2)}) collective-permute-start(bf16[128,384]{1,0:T(8,128)(2,1)} %param.13), channel_id=1, source_target_pairs={{0,0},{128,1},{2,2},{130,3},{4,4},{132,5},{6,6},{134,7},{8,8},{136... | collective-permute-start | bytes 294920 | tf_op jit(solution)/shard_map/ppermute | solution.py:43
  5.6 4.5 %collective-permute-start.5 = (bf16[128,384]{1,0:T(8,128)(2,1)}, bf16[128,384]{1,0:T(8,128)(2,1)S(1)}, u32[]{:S(2)}, u32[]{:S(2)}) collective-permute-start(bf16[128,384]{1,0:T(8,128)(2,1)} %param.13), channel_id=1, source_target_pairs={{8,0},{136,1},{10,2},{138,3},{12,4},{140,5},{14,6},{142,7},{16,8},... | collective-permute-start | bytes 294920 | tf_op jit(solution)/shard_map/ppermute | solution.py:43
  10.0 2.2 collective-permute-start.6
  13.6 4.3 %pack.1 = bf16[16,768,128]{2,1,0:T(8,128)(2,1)} custom-call(bf16[1,2,128,6144]{3,2,1,0:T(8,128)(2,1)} %q_ref.3, bf16[1,2,128,6144]{3,2,1,0:T(8,128)(2,1)} %q_ref.3, bf16[1,2,32,4096]{3,2,1,0:T(8,128)(2,1)} %vt_ref.1, bf16[1,2,32,4096]{3,2,1,0:T(8,128)(2,1)} %vt_ref.1, bf16[1,2,128,6144]{3,2,1,0:T(8,128)(2,1)} %q_ref.3), custom_call_target="tpu_custom_call" | custom-call | bytes 6291456 | tf_op jit(solution)/shard_map/pack/pallas_call | solution.py:102
  17.9 2.2 collective-permute-done.6
  21.6 7.5 %all-to-all-start = ((bf16[16,768,128]{2,1,0:T(8,128)(2,1)}), bf16[16,768,128]{2,1,0:T(8,128)(2,1)}, u32[]{:S(2)}, u32[]{:S(2)}) async-start(bf16[16,768,128]{2,1,0:T(8,128)(2,1)} %pack.1), calls=%async_computation | async-start | bytes 6291456 | tf_op jit(solution)/shard_map/all_to_all | solution.py:352
  29.3 3.0 %collective-permute-start = (f32[8]{0:T(128)S(1)}, f32[8]{0:T(128)S(1)}, u32[]{:S(2)}, u32[]{:S(2)}) collective-permute-start(f32[8]{0:T(128)S(1)} %select_reduce_fusion.1), channel_id=1, source_target_pairs={{4,0},{5,1},{6,2},{7,3},{0,4},{1,5},{2,6},{3,7},{12,8},{13,9},{14,... | collective-permute-start | bytes 104 | tf_op jit(solution)/shard_map/ppermute | solution.py:53
  34.6 2.4 collective-permute-done.2
  37.0 2.5 %collective-permute-start.8 = (bf16[512,384]{1,0:T(8,128)(2,1)S(1)}, bf16[512,384]{1,0:T(8,128)(2,1)S(1)}, u32[]{:S(2)}, u32[]{:S(2)}) collective-permute-start(bf16[512,384]{1,0:T(8,128)(2,1)S(1)} %constant_dynamic-update-slice_fusion), channel_id=1, source_target_pairs={{32,0},{40,8},{48,16},{56,24},{64,32},{72,40},{80,48},{88,56},{96,... | collective-permute-start | bytes 1179656 | tf_op jit(solution)/shard_map/ppermute | solution.py:28
  41.5 9.5 %collective-permute-done.8 = bf16[512,384]{1,0:T(8,128)(2,1)S(1)} collective-permute-done((bf16[512,384]{1,0:T(8,128)(2,1)S(1)}, bf16[512,384]{1,0:T(8,128)(2,1)S(1)}, u32[]{:S(2)}, u32[]{:S(2)}) %collective-permute-start.8) | collective-permute-done | bytes 393248 | tf_op jit(solution)/shard_map/ppermute | solution.py:28
  54.5 12.7 %collective-permute-done.10 = bf16[512,384]{1,0:T(8,128)(2,1)S(1)} collective-permute-done((bf16[512,384]{1,0:T(8,128)(2,1)S(1)}, bf16[512,384]{1,0:T(8,128)(2,1)S(1)}, u32[]{:S(2)}, u32[]{:S(2)}) %collective-permute-start.10) | collective-permute-done | bytes 393248 | tf_op jit(solution)/shard_map/ppermute | solution.py:28
  68.5 2.3 collective-permute-start.12
  72.9 28.9 %all-to-all-done.q_ref.kv_ref = bf16[16,768,128]{2,1,0:T(8,128)(2,1)} async-done(((bf16[16,768,128]{2,1,0:T(8,128)(2,1)}), bf16[16,768,128]{2,1,0:T(8,128)(2,1)}, u32[]{:S(2)}, u32[]{:S(2)}) %all-to-all-start) | async-done | bytes 3145760 | tf_op jit(solution)/shard_map/all_to_all | solution.py:352
  101.9 8.9 %all-to-all-start.1 = ((bf16[16,128,128]{2,1,0:T(8,128)(2,1)}), bf16[16,128,128]{2,1,0:T(8,128)(2,1)S(1)}, u32[]{:S(2)}, u32[]{:S(2)}) async-start(bf16[16,128,128]{2,1,0:T(8,128)(2,1)} %pack_queries.1), calls=%async_computation.1 | async-start | bytes 1048576 | tf_op jit(solution)/shard_map/all_to_all | solution.py:352
  110.7 9.2 %attention0.1.rest_0_ = bf16[16,256,128]{2,1,0:T(8,128)(2,1)} custom-call(bf16[16,768,128]{2,1,0:T(8,128)(2,1)} %all-to-all-done.q_ref.kv_ref, bf16[16,768,128]{2,1,0:T(8,128)(2,1)} %all-to-all-done.q_ref.kv_ref), custom_call_target="tpu_custom_call" | custom-call | flops 5368709120 | bytes 2359296 | tf_op jit(solution)/shard_map/attention0/pallas_call | solution.py:162
  119.9 6.3 %all-to-all-done.1.q_ref = bf16[16,128,128]{2,1,0:T(8,128)(2,1)S(1)} async-done(((bf16[16,128,128]{2,1,0:T(8,128)(2,1)}), bf16[16,128,128]{2,1,0:T(8,128)(2,1)S(1)}, u32[]{:S(2)}, u32[]{:S(2)}) %all-to-all-start.1) | async-done | bytes 524320 | tf_op jit(solution)/shard_map/all_to_all | solution.py:352
  127.0 23.0 %attention1.1 = bf16[16,256,128]{2,1,0:T(8,128)(2,1)} custom-call(bf16[16,128,128]{2,1,0:T(8,128)(2,1)} %copy-done.9, bf16[16,768,128]{2,1,0:T(8,128)(2,1)} %all-to-all-done.q_ref.kv_ref, bf16[16,256,128]{2,1,0:T(8,128)(2,1)} %attention0.1.rest_0_), custom_call_target="tpu_custom_call", output_to_operand_aliasing={{}: (2, {})} | custom-call | flops 5368709120 | bytes 2359296 | tf_op jit(solution)/shard_map/attention1/pallas_call | solution.py:162
  150.1 3.7 %all-to-all-start.2 = ((bf16[16,256,128]{2,1,0:T(8,128)(2,1)}), bf16[16,256,128]{2,1,0:T(8,128)(2,1)S(1)}, u32[]{:S(2)}, u32[]{:S(2)}) async-start(bf16[16,256,128]{2,1,0:T(8,128)(2,1)} %attention1.1), calls=%async_computation.2 | async-start | bytes 2097152 | tf_op jit(solution)/shard_map/all_to_all | solution.py:352
  154.7 2.8 %collective-permute-start.14 = (bf16[1024,384]{1,0:T(8,128)(2,1)}, bf16[1024,384]{1,0:T(8,128)(2,1)S(1)}, u32[]{:S(2)}, u32[]{:S(2)}) collective-permute-start(bf16[1024,384]{1,0:T(8,128)(2,1)} %slice.20), channel_id=1, source_target_pairs={{2,0},{3,1},{4,2},{5,3},{6,4},{7,5},{0,6},{1,7},{10,8},{11,9},{12,... | collective-permute-start | bytes 2359304 | tf_op jit(solution)/shard_map/ppermute | solution.py:53
  157.5 2.1 slice.21
  161.4 11.7 %collective-permute-done.14.rest_3_ = bf16[1024,384]{1,0:T(8,128)(2,1)S(1)} collective-permute-done((bf16[1024,384]{1,0:T(8,128)(2,1)}, bf16[1024,384]{1,0:T(8,128)(2,1)S(1)}, u32[]{:S(2)}, u32[]{:S(2)}) %collective-permute-start.14) | collective-permute-done | bytes 786464 | tf_op jit(solution)/shard_map/ppermute | solution.py:53
  173.1 2.5 %collective-permute-start.18 = (bf16[1024,384]{1,0:T(8,128)(2,1)S(1)}, bf16[1024,384]{1,0:T(8,128)(2,1)}, u32[]{:S(2)}, u32[]{:S(2)}) collective-permute-start(bf16[1024,384]{1,0:T(8,128)(2,1)S(1)} %collective-permute-done.14.rest_3_), channel_id=1, source_target_pairs={{0,128},{128,0},{1,129},{129,1},{2,130},{130,2},{3,131},{131,3},{4... | collective-permute-start | bytes 2359304 | tf_op jit(solution)/shard_map/ppermute | solution.py:62
  175.6 2.8 %collective-permute-done.15.rest_4_ = bf16[1024,384]{1,0:T(8,128)(2,1)} collective-permute-done((bf16[1024,384]{1,0:T(8,128)(2,1)}, bf16[1024,384]{1,0:T(8,128)(2,1)}, u32[]{:S(2)}, u32[]{:S(2)}) %collective-permute-start.15) | collective-permute-done | bytes 786464 | tf_op jit(solution)/shard_map/ppermute | solution.py:53
  178.3 2.7 %collective-permute-start.19 = (bf16[1024,384]{1,0:T(8,128)(2,1)}, bf16[1024,384]{1,0:T(8,128)(2,1)}, u32[]{:S(2)}, u32[]{:S(2)}) collective-permute-start(bf16[1024,384]{1,0:T(8,128)(2,1)} %collective-permute-done.15.rest_4_), channel_id=1, source_target_pairs={{0,128},{128,0},{1,129},{129,1},{2,130},{130,2},{3,131},{131,3},{4... | collective-permute-start | bytes 2359304 | tf_op jit(solution)/shard_map/ppermute | solution.py:62
  188.0 9.8 %hidden.1 = (bf16[256,3072]{1,0:T(8,128)(2,1)S(1)}, f32[64,256]{1,0:T(8,128)S(1)}) custom-call(s32[4]{0:T(128)S(1)} %pad_add_fusion.place, bf16[16,256,128]{2,1,0:T(8,128)(2,1)S(1)} %all-to-all-done.2.heads_ref, bf16[1,2,128,3072]{3,2,1,0:T(8,128)(2,1)S(1)} %copy-done.1, bf16[3,2,3072]{2,1,0:T(2,128)(2,1)S(1)} %bitcast.21, bf16[64,3072]{1,0:T(8,128)(2,1)S(1)} %bitcast.18, ...), custom_call_target="tpu_custom_call" | custom-call | flops 3221225472 | bytes 12582912 | tf_op jit(solution)/shard_map/hidden/pallas_call | solution.py:250
  202.9 11.8 %all_to_all.20.parts_ref = f32[8,32,384]{2,1,0:T(8,128)} all-to-all(f32[8,32,384]{2,1,0:T(8,128)S(1)} %add.49), channel_id=1, replica_groups=mesh['cfg'=2,'seq'=16,'dp'=8] {'dp'}, dimensions={0} | all-to-all | bytes 786432 | tf_op jit(solution)/shard_map/all_to_all | solution.py:435
  216.3 4.6 %collective-permute-start.22 = (f32[40,384]{1,0:T(8,128)}, f32[40,384]{1,0:T(8,128)S(1)}, u32[]{:S(2)}, u32[]{:S(2)}) collective-permute-start(f32[40,384]{1,0:T(8,128)} %fold.1), channel_id=1, source_target_pairs={{16,0},{24,8},{0,16},{8,24},{48,32},{56,40},{32,48},{40,56},{80,64... | collective-permute-start | bytes 184328 | tf_op jit(solution)/shard_map/ppermute | solution.py:48
  221.2 2.1 collective-permute-start.24
  223.6 4.5 %collective-permute-done.23 = f32[40,384]{1,0:T(8,128)S(1)} collective-permute-done((f32[40,384]{1,0:T(8,128)}, f32[40,384]{1,0:T(8,128)S(1)}, u32[]{:S(2)}, u32[]{:S(2)}) %collective-permute-start.23) | collective-permute-done | bytes 61472 | tf_op jit(solution)/shard_map/ppermute | solution.py:48
  229.0 2.8 %collective-permute-start.25 = (f32[40,384]{1,0:T(8,128)S(1)}, f32[40,384]{1,0:T(8,128)S(1)}, u32[]{:S(2)}, u32[]{:S(2)}) collective-permute-start(f32[40,384]{1,0:T(8,128)S(1)} %add_add_fusion.1), channel_id=1, source_target_pairs={{64,0},{72,8},{80,16},{88,24},{96,32},{104,40},{112,48},{120,56},{... | collective-permute-start | bytes 184328 | tf_op jit(solution)/shard_map/ppermute | solution.py:28
  234.8 2.4 collective-permute-done.27
  237.3 3.0 %collective-permute-start.28 = (f32[40,384]{1,0:T(8,128)S(1)}, f32[40,384]{1,0:T(8,128)S(1)}, u32[]{:S(2)}, u32[]{:S(2)}) collective-permute-start(f32[40,384]{1,0:T(8,128)S(1)} %add_add_fusion), channel_id=1, source_target_pairs={{0,128},{128,0},{1,129},{129,1},{2,130},{130,2},{3,131},{131,3},{4... | collective-permute-start | bytes 184328 | tf_op jit(solution)/shard_map/ppermute | solution.py:62
  (92 shorter events, 37.6 us)
Async XLA Ops:
  0.6 17.2 %collective-permute-start.4 = (bf16[128,384]{1,0:T(8,128)(2,1)}, bf16[128,384]{1,0:T(8,128)(2,1)S(1)}, u32[]{:S(2)}, u32[]{:S(2)}) collective-permute-start(bf16[128,384]{1,0:T(8,128)(2,1)} %param.13), channel_id=1, source_target_pairs={{0,0},{128,1},{2,2},{130,3},{4,4},{132,5},{6,6},{134,7},{8,8},{136... | collective-permute-start | bytes 294920 | tf_op jit(solution)/shard_map/ppermute | solution.py:43
  5.6 12.4 %collective-permute-start.5 = (bf16[128,384]{1,0:T(8,128)(2,1)}, bf16[128,384]{1,0:T(8,128)(2,1)S(1)}, u32[]{:S(2)}, u32[]{:S(2)}) collective-permute-start(bf16[128,384]{1,0:T(8,128)(2,1)} %param.13), channel_id=1, source_target_pairs={{8,0},{136,1},{10,2},{138,3},{12,4},{140,5},{14,6},{142,7},{16,8},... | collective-permute-start | bytes 294920 | tf_op jit(solution)/shard_map/ppermute | solution.py:43
  10.0 10.1 %collective-permute-start.6 = (bf16[128,384]{1,0:T(8,128)(2,1)}, bf16[128,384]{1,0:T(8,128)(2,1)S(1)}, u32[]{:S(2)}, u32[]{:S(2)}) collective-permute-start(bf16[128,384]{1,0:T(8,128)(2,1)} %param.13), channel_id=1, source_target_pairs={{16,0},{144,1},{18,2},{146,3},{20,4},{148,5},{22,6},{150,7},{24,8}... | collective-permute-start | bytes 294920 | tf_op jit(solution)/shard_map/ppermute | solution.py:43
  12.2 9.4 %collective-permute-start.7 = (bf16[128,384]{1,0:T(8,128)(2,1)}, bf16[128,384]{1,0:T(8,128)(2,1)S(1)}, u32[]{:S(2)}, u32[]{:S(2)}) collective-permute-start(bf16[128,384]{1,0:T(8,128)(2,1)} %param.13), channel_id=1, source_target_pairs={{24,0},{152,1},{26,2},{154,3},{28,4},{156,5},{30,6},{158,7},{0,8},... | collective-permute-start | bytes 294920 | tf_op jit(solution)/shard_map/ppermute | solution.py:43
  21.6 80.2 %all-to-all-start = ((bf16[16,768,128]{2,1,0:T(8,128)(2,1)}), bf16[16,768,128]{2,1,0:T(8,128)(2,1)}, u32[]{:S(2)}, u32[]{:S(2)}) async-start(bf16[16,768,128]{2,1,0:T(8,128)(2,1)} %pack.1), calls=%async_computation | async-start | bytes 6291456 | tf_op jit(solution)/shard_map/all_to_all | solution.py:352
  29.3 4.4 %collective-permute-start = (f32[8]{0:T(128)S(1)}, f32[8]{0:T(128)S(1)}, u32[]{:S(2)}, u32[]{:S(2)}) collective-permute-start(f32[8]{0:T(128)S(1)} %select_reduce_fusion.1), channel_id=1, source_target_pairs={{4,0},{5,1},{6,2},{7,3},{0,4},{1,5},{2,6},{3,7},{12,8},{13,9},{14,... | collective-permute-start | bytes 104 | tf_op jit(solution)/shard_map/ppermute | solution.py:53
  32.2 2.4 collective-permute-start.1
  33.0 4.0 %collective-permute-start.2 = (f32[8]{0:T(128)S(1)}, f32[8]{0:T(128)S(1)}, u32[]{:S(2)}, u32[]{:S(2)}) collective-permute-start(f32[8]{0:T(128)S(1)} %select_reduce_fusion.1), channel_id=1, source_target_pairs={{6,0},{7,1},{0,2},{1,3},{2,4},{3,5},{4,6},{5,7},{14,8},{15,9},{8,1... | collective-permute-start | bytes 104 | tf_op jit(solution)/shard_map/ppermute | solution.py:53
  37.0 13.9 %collective-permute-start.8 = (bf16[512,384]{1,0:T(8,128)(2,1)S(1)}, bf16[512,384]{1,0:T(8,128)(2,1)S(1)}, u32[]{:S(2)}, u32[]{:S(2)}) collective-permute-start(bf16[512,384]{1,0:T(8,128)(2,1)S(1)} %constant_dynamic-update-slice_fusion), channel_id=1, source_target_pairs={{32,0},{40,8},{48,16},{56,24},{64,32},{72,40},{80,48},{88,56},{96,... | collective-permute-start | bytes 1179656 | tf_op jit(solution)/shard_map/ppermute | solution.py:28
  39.5 14.2 %collective-permute-start.9 = (bf16[512,384]{1,0:T(8,128)(2,1)S(1)}, bf16[512,384]{1,0:T(8,128)(2,1)S(1)}, u32[]{:S(2)}, u32[]{:S(2)}) collective-permute-start(bf16[512,384]{1,0:T(8,128)(2,1)S(1)} %constant_dynamic-update-slice_fusion), channel_id=1, source_target_pairs={{64,0},{72,8},{80,16},{88,24},{96,32},{104,40},{112,48},{120,56},{... | collective-permute-start | bytes 1179656 | tf_op jit(solution)/shard_map/ppermute | solution.py:28
  40.1 27.2 %collective-permute-start.10 = (bf16[512,384]{1,0:T(8,128)(2,1)S(1)}, bf16[512,384]{1,0:T(8,128)(2,1)S(1)}, u32[]{:S(2)}, u32[]{:S(2)}) collective-permute-start(bf16[512,384]{1,0:T(8,128)(2,1)S(1)} %constant_dynamic-update-slice_fusion), channel_id=1, source_target_pairs={{96,0},{104,8},{112,16},{120,24},{0,32},{8,40},{16,48},{24,56},{32... | collective-permute-start | bytes 1179656 | tf_op jit(solution)/shard_map/ppermute | solution.py:28
  68.1 3.7 %collective-permute-start.11 = (bf16[2048,384]{1,0:T(8,128)(2,1)}, bf16[2048,384]{1,0:T(8,128)(2,1)S(1)}, u32[]{:S(2)}, u32[]{:S(2)}) collective-permute-start(bf16[2048,384]{1,0:T(8,128)(2,1)} %constant_dynamic-update-slice_fusion.4.rest_0_), channel_id=1, source_target_pairs={{0,128},{128,0},{1,129},{129,1},{2,130},{130,2},{3,131},{131,3},{4... | collective-permute-start | bytes 4718600 | tf_op jit(solution)/shard_map/ppermute | solution.py:62
  68.5 51.4 %collective-permute-start.12 = (bf16[2048,384]{1,0:T(8,128)(2,1)}, bf16[2048,384]{1,0:T(8,128)(2,1)S(1)}, u32[]{:S(2)}, u32[]{:S(2)}) collective-permute-start(bf16[2048,384]{1,0:T(8,128)(2,1)} %constant_dynamic-update-slice_fusion.4.rest_0_), channel_id=1, source_target_pairs={{2,0},{3,1},{4,2},{5,3},{6,4},{7,5},{0,6},{1,7},{10,8},{11,9},{12,... | collective-permute-start | bytes 4718600 | tf_op jit(solution)/shard_map/ppermute | solution.py:53
  70.8 49.1 %collective-permute-start.13 = (bf16[2048,384]{1,0:T(8,128)(2,1)}, bf16[2048,384]{1,0:T(8,128)(2,1)}, u32[]{:S(2)}, u32[]{:S(2)}) collective-permute-start(bf16[2048,384]{1,0:T(8,128)(2,1)} %constant_dynamic-update-slice_fusion.4.rest_0_), channel_id=1, source_target_pairs={{6,0},{7,1},{0,2},{1,3},{2,4},{3,5},{4,6},{5,7},{14,8},{15,9},{8,1... | collective-permute-start | bytes 4718600 | tf_op jit(solution)/shard_map/ppermute | solution.py:53
  101.9 24.4 %all-to-all-start.1 = ((bf16[16,128,128]{2,1,0:T(8,128)(2,1)}), bf16[16,128,128]{2,1,0:T(8,128)(2,1)S(1)}, u32[]{:S(2)}, u32[]{:S(2)}) async-start(bf16[16,128,128]{2,1,0:T(8,128)(2,1)} %pack_queries.1), calls=%async_computation.1 | async-start | bytes 1048576 | tf_op jit(solution)/shard_map/all_to_all | solution.py:352
  150.1 34.1 %all-to-all-start.2 = ((bf16[16,256,128]{2,1,0:T(8,128)(2,1)}), bf16[16,256,128]{2,1,0:T(8,128)(2,1)S(1)}, u32[]{:S(2)}, u32[]{:S(2)}) async-start(bf16[16,256,128]{2,1,0:T(8,128)(2,1)} %attention1.1), calls=%async_computation.2 | async-start | bytes 2097152 | tf_op jit(solution)/shard_map/all_to_all | solution.py:352
  154.7 18.4 %collective-permute-start.14 = (bf16[1024,384]{1,0:T(8,128)(2,1)}, bf16[1024,384]{1,0:T(8,128)(2,1)S(1)}, u32[]{:S(2)}, u32[]{:S(2)}) collective-permute-start(bf16[1024,384]{1,0:T(8,128)(2,1)} %slice.20), channel_id=1, source_target_pairs={{2,0},{3,1},{4,2},{5,3},{6,4},{7,5},{0,6},{1,7},{10,8},{11,9},{12,... | collective-permute-start | bytes 2359304 | tf_op jit(solution)/shard_map/ppermute | solution.py:53
  159.6 18.7 %collective-permute-start.15 = (bf16[1024,384]{1,0:T(8,128)(2,1)}, bf16[1024,384]{1,0:T(8,128)(2,1)}, u32[]{:S(2)}, u32[]{:S(2)}) collective-permute-start(bf16[1024,384]{1,0:T(8,128)(2,1)} %slice.21), channel_id=1, source_target_pairs={{6,0},{7,1},{0,2},{1,3},{2,4},{3,5},{4,6},{5,7},{14,8},{15,9},{8,1... | collective-permute-start | bytes 2359304 | tf_op jit(solution)/shard_map/ppermute | solution.py:53
  159.6 24.6 %collective-permute-start.16 = (bf16[2048,384]{1,0:T(8,128)(2,1)S(1)}, bf16[2048,384]{1,0:T(8,128)(2,1)}, u32[]{:S(2)}, u32[]{:S(2)}) collective-permute-start(bf16[2048,384]{1,0:T(8,128)(2,1)S(1)} %collective-permute-done.12.rest_1_), channel_id=1, source_target_pairs={{0,128},{128,0},{1,129},{129,1},{2,130},{130,2},{3,131},{131,3},{4... | collective-permute-start | bytes 4718600 | tf_op jit(solution)/shard_map/ppermute | solution.py:62
  161.4 22.8 %collective-permute-start.17 = (bf16[2048,384]{1,0:T(8,128)(2,1)}, bf16[2048,384]{1,0:T(8,128)(2,1)}, u32[]{:S(2)}, u32[]{:S(2)}) collective-permute-start(bf16[2048,384]{1,0:T(8,128)(2,1)} %collective-permute-done.13.rest_2_), channel_id=1, source_target_pairs={{0,128},{128,0},{1,129},{129,1},{2,130},{130,2},{3,131},{131,3},{4... | collective-permute-start | bytes 4718600 | tf_op jit(solution)/shard_map/ppermute | solution.py:62
  173.1 11.1 %collective-permute-start.18 = (bf16[1024,384]{1,0:T(8,128)(2,1)S(1)}, bf16[1024,384]{1,0:T(8,128)(2,1)}, u32[]{:S(2)}, u32[]{:S(2)}) collective-permute-start(bf16[1024,384]{1,0:T(8,128)(2,1)S(1)} %collective-permute-done.14.rest_3_), channel_id=1, source_target_pairs={{0,128},{128,0},{1,129},{129,1},{2,130},{130,2},{3,131},{131,3},{4... | collective-permute-start | bytes 2359304 | tf_op jit(solution)/shard_map/ppermute | solution.py:62
  178.3 5.8 %collective-permute-start.19 = (bf16[1024,384]{1,0:T(8,128)(2,1)}, bf16[1024,384]{1,0:T(8,128)(2,1)}, u32[]{:S(2)}, u32[]{:S(2)}) collective-permute-start(bf16[1024,384]{1,0:T(8,128)(2,1)} %collective-permute-done.15.rest_4_), channel_id=1, source_target_pairs={{0,128},{128,0},{1,129},{129,1},{2,130},{130,2},{3,131},{131,3},{4... | collective-permute-start | bytes 2359304 | tf_op jit(solution)/shard_map/ppermute | solution.py:62
  181.1 2.8 %collective-permute-start.3 = (f32[8]{0:T(128)S(1)}, f32[8]{0:T(128)S(1)}, u32[]{:S(2)}, u32[]{:S(2)}) collective-permute-start(f32[8]{0:T(128)S(1)} %add_add_fusion.2), channel_id=1, source_target_pairs={{1,0},{0,1},{3,2},{2,3},{5,4},{4,5},{7,6},{6,7},{9,8},{8,9},{11,10... | collective-permute-start | bytes 104 | tf_op jit(solution)/shard_map/ppermute | solution.py:58
  197.8 2.2 collective-permute-start.20
  201.0 1.8 collective-permute-start.21
  216.3 7.3 %collective-permute-start.22 = (f32[40,384]{1,0:T(8,128)}, f32[40,384]{1,0:T(8,128)S(1)}, u32[]{:S(2)}, u32[]{:S(2)}) collective-permute-start(f32[40,384]{1,0:T(8,128)} %fold.1), channel_id=1, source_target_pairs={{16,0},{24,8},{0,16},{8,24},{48,32},{56,40},{32,48},{40,56},{80,64... | collective-permute-start | bytes 184328 | tf_op jit(solution)/shard_map/ppermute | solution.py:48
  220.9 7.2 %collective-permute-start.23 = (f32[40,384]{1,0:T(8,128)}, f32[40,384]{1,0:T(8,128)S(1)}, u32[]{:S(2)}, u32[]{:S(2)}) collective-permute-start(f32[40,384]{1,0:T(8,128)} %fold.1), channel_id=1, source_target_pairs={{8,0},{16,8},{24,16},{0,24},{40,32},{48,40},{56,48},{32,56},{72,64... | collective-permute-start | bytes 184328 | tf_op jit(solution)/shard_map/ppermute | solution.py:48
  221.2 6.9 %collective-permute-start.24 = (f32[40,384]{1,0:T(8,128)}, f32[40,384]{1,0:T(8,128)S(1)}, u32[]{:S(2)}, u32[]{:S(2)}) collective-permute-start(f32[40,384]{1,0:T(8,128)} %fold.1), channel_id=1, source_target_pairs={{24,0},{0,8},{8,16},{16,24},{56,32},{32,40},{40,48},{48,56},{88,64... | collective-permute-start | bytes 184328 | tf_op jit(solution)/shard_map/ppermute | solution.py:48
  229.0 4.7 %collective-permute-start.25 = (f32[40,384]{1,0:T(8,128)S(1)}, f32[40,384]{1,0:T(8,128)S(1)}, u32[]{:S(2)}, u32[]{:S(2)}) collective-permute-start(f32[40,384]{1,0:T(8,128)S(1)} %add_add_fusion.1), channel_id=1, source_target_pairs={{64,0},{72,8},{80,16},{88,24},{96,32},{104,40},{112,48},{120,56},{... | collective-permute-start | bytes 184328 | tf_op jit(solution)/shard_map/ppermute | solution.py:28
  231.8 3.1 %collective-permute-start.26 = (f32[40,384]{1,0:T(8,128)S(1)}, f32[40,384]{1,0:T(8,128)S(1)}, u32[]{:S(2)}, u32[]{:S(2)}) collective-permute-start(f32[40,384]{1,0:T(8,128)S(1)} %add_add_fusion.1), channel_id=1, source_target_pairs={{32,0},{40,8},{48,16},{56,24},{64,32},{72,40},{80,48},{88,56},{96,... | collective-permute-start | bytes 184328 | tf_op jit(solution)/shard_map/ppermute | solution.py:28
  232.7 4.6 %collective-permute-start.27 = (f32[40,384]{1,0:T(8,128)S(1)}, f32[40,384]{1,0:T(8,128)S(1)}, u32[]{:S(2)}, u32[]{:S(2)}) collective-permute-start(f32[40,384]{1,0:T(8,128)S(1)} %add_add_fusion.1), channel_id=1, source_target_pairs={{96,0},{104,8},{112,16},{120,24},{0,32},{8,40},{16,48},{24,56},{32... | collective-permute-start | bytes 184328 | tf_op jit(solution)/shard_map/ppermute | solution.py:28
  237.3 3.9 %collective-permute-start.28 = (f32[40,384]{1,0:T(8,128)S(1)}, f32[40,384]{1,0:T(8,128)S(1)}, u32[]{:S(2)}, u32[]{:S(2)}) collective-permute-start(f32[40,384]{1,0:T(8,128)S(1)} %add_add_fusion), channel_id=1, source_target_pairs={{0,128},{128,0},{1,129},{129,1},{2,130},{130,2},{3,131},{131,3},{4... | collective-permute-start | bytes 184328 | tf_op jit(solution)/shard_map/ppermute | solution.py:62
  (13 other events, 118.7 us)
where the time goes:
time: 243 us; the launch traced here: 242 us
  waiting for transfers between devices  93.6 us (39%)
  starting transfers between devices  71 us (29%)
  Pallas kernels  49.8 us (20%)
  local copies, waits for them, and re-layouts  12.1 us (5%)
  blocking collectives  11.8 us (5%)
  other arithmetic  2.61 us (1%)
    all_to_all x3, waiting for transfers between devices, exchange(): return lax.all_to_all(send, 'seq', split_axis=0, concat_axis=0, tiled=True)  35.2 us
    pallas_call x2, Pallas kernels, attention(): pl.pallas_call(attention_kernel, grid=(1,), in_specs=[pl.BlockSpec((peers...  32.2 us
    ppermute x6, waiting for transfers between devices, from_x(): return lax.ppermute(value, 'seq', pairs)  28.2 us
    all_to_all x3, starting transfers between devices, exchange(): return lax.all_to_all(send, 'seq', split_axis=0, concat_axis=0, tiled=True)  20 us
    ppermute x7, waiting for transfers between devices, from_y(): return lax.ppermute(value, 'dp', pairs)  17.8 us
    ppermute x4, starting transfers between devices, from_column(): return lax.ppermute(value, ('cfg', 'seq', 'dp'), pairs)  12.9 us
    ppermute x8, starting transfers between devices, from_cfg(): return lax.ppermute(value, 'cfg', [(0, 1), (1, 0)])  12.2 us
    all_to_all x1, blocking collectives, per_device(): lax.all_to_all(kept, 'dp', split_axis=0, concat_axis=0, tiled=True)  11.8 us
  transfers between devices with their start and end apart: 32, of which 20 were waited for; matrix products, arithmetic and copies ran while one was open for 3% of the time, Pallas kernels for 6%

commit v1 on v0

--- a/solution.py
+++ b/solution.py
@@ -184,24 +184,33 @@
     )(queries, key_values, *earlier)
 
 
-def hidden_kernel(place, heads_ref, state_ref, mods_ref, final_ref, *rest):
-    pieces, (hidden_ref, velocity_ref, flat, mixed, weights, sems) = rest[:10], rest[10:]
+SPANS = ((0, 0), (0, 1), (1, 0), (1, 1), (3, 0), (3, 1), (2, 0), (2, 1), (2, 2))
+
+
+def hidden_kernel(place, heads_ref, state_any, mods_any, final_any, *rest):
+    pieces = rest[: 2 * len(SPANS)]
+    hidden_ref, velocity_ref, flat, mixed, weights, state_ref, mods_ref, final_ref, sems = rest[
+        2 * len(SPANS) :
+    ]
     x_at, zh_at, y_at, c_at = place[0], place[1], place[2], place[3]
     per_dev, rows = state_ref.shape[1], state_ref.shape[2]
     width = weights.shape[2]
-    depth = weights.shape[1]
-    spans = ((0, 0), (1, 0), (3, 0), (2, 0), (2, depth // 2))
+    part = weights.shape[1] // X
+
+    def begin(source, target, n):
+        copy = pltpu.make_async_copy(source, target, sems.at[n])
+        copy.start()
+        return copy
+
     copies = []
-    for core in range(2):
-        for n, (turn, at_row) in enumerate(spans):
-            piece = pieces[core * 5 + n]
-            copy = pltpu.make_async_copy(
-                piece,
-                weights.at[core * 4 + turn, pl.ds(at_row, piece.shape[0])],
-                sems.at[core * 5 + n],
-            )
-            copy.start()
-            copies.append(copy)
+    for n, piece in enumerate(pieces):
+        core, (turn, first) = n // len(SPANS), SPANS[n % len(SPANS)]
+        target = weights.at[core * Y + turn, pl.ds(first * part, piece.shape[0])]
+        copies.append(begin(piece, target, n))
+        if n == 1:
+            mods_copy = begin(mods_any, mods_ref, len(pieces))
+            state_copy = begin(state_any, state_ref, len(pieces) + 1)
+    final_copy = begin(final_any, final_ref, len(pieces) + 2)
     for i in range(X):
         for j in range(ZH):
             head = lax.rem(x_at + i, X) * ZH + lax.rem(zh_at + j, ZH)
@@ -211,13 +220,17 @@
     square_sum = jnp.zeros((per_dev * rows, 1), jnp.float32)
     for core in range(2):
         core_at = c_at if core == 0 else 1 - c_at
-        for turn, needed in ((0, (0,)), (1, (1,)), (3, (2,)), (2, (3, 4))):
-            for n in needed:
-                copies[core * 5 + n].wait()
+        for turn in (0, 1, 3, 2):
+            for n, (of_turn, _) in enumerate(SPANS):
+                if of_turn == turn:
+                    copies[core * len(SPANS) + n].wait()
             at = pl.ds(pl.multiple_of((lax.rem(y_at + turn, Y) * ZL + core_at) * width, 128), width)
             projected = jnp.dot(
-                flat[...], weights[core * 4 + turn], preferred_element_type=jnp.float32
+                flat[...], weights[core * Y + turn], preferred_element_type=jnp.float32
             )
+            if core == 0 and turn == 0:
+                mods_copy.wait()
+                state_copy.wait()
             for r in range(per_dev):
                 gate = mods_ref[0, r : r + 1, at].astype(jnp.float32)
                 mixed[r * rows : (r + 1) * rows, at] = (
@@ -238,6 +251,7 @@
         hidden_ref[at, :] = (
             (mixed[at, :] - center[at]) * inverse[at] * scale + shift
         ).astype(jnp.bfloat16)
+    final_copy.wait()
     velocity_ref[...] = lax.dot_general(
         final_ref[...], hidden_ref[...], (((1,), (1,)), ((), ())), preferred_element_type=jnp.float32
     )
@@ -250,8 +264,8 @@
     return pl.pallas_call(
         hidden_kernel,
         in_specs=[pl.BlockSpec(memory_space=pltpu.SMEM)]
-        + [vmem] * 4
-        + [pl.BlockSpec(memory_space=pl.ANY)] * 10,
+        + [vmem]
+        + [pl.BlockSpec(memory_space=pl.ANY)] * (3 + len(pieces)),
         out_specs=[vmem] * 2,
         out_shape=[
             jax.ShapeDtypeStruct((all_rows, width_all), jnp.bfloat16),
@@ -261,7 +275,10 @@
             pltpu.VMEM((all_rows, heads * HD), jnp.bfloat16),
             pltpu.VMEM((all_rows, width_all), jnp.float32),
             pltpu.VMEM((8, heads * HD, pieces[0].shape[1]), jnp.bfloat16),
-            pltpu.SemaphoreType.DMA((10,)),
+            pltpu.VMEM(image_state.shape, jnp.bfloat16),
+            pltpu.VMEM(modulation.shape, jnp.bfloat16),
+            pltpu.VMEM(final_weight.shape, jnp.bfloat16),
+            pltpu.SemaphoreType.DMA((len(pieces) + 3,)),
         ],
         compiler_params=pltpu.CompilerParams(vmem_limit_bytes=HIDDEN_VMEM_BYTES),
         cost_estimate=pl.CostEstimate(
@@ -381,24 +398,29 @@
     member = (group_index[:, None] == jnp.arange(group_count, dtype=jnp.int32)[None, :]).astype(
         jnp.float32
     )
-    column = jnp.concatenate([from_column(output_weight, d) for d in range(ZH)], axis=0)
+    packed = pack(image_projections, text_projections)
+    columns = after(output_weight, packed)
+    column = jnp.concatenate([from_column(columns, d) for d in range(ZH)], axis=0)
+    first_part = exchange(after(packed, column))
+    depth = column.shape[0]
+    ahead_own, behind_own = from_y(column, 1), from_y(column, -1)
+    others = jnp.concatenate([from_x(column, d) for d in range(1, X)], axis=0)
+    far_own = from_y(ahead_own, 1)
     totals = jnp.sum(member * rewards[:, None], axis=0)
-    first_part = exchange(after(pack(image_projections, text_projections), column))
     totals = ring_sum(totals, from_y)
-    column = after(column, totals)
-    totals = totals + from_zl(totals)
-    advantage = rewards - jnp.sum(member * totals[None, :], axis=1) / GROUP_SIZE
-    plane = jnp.concatenate([column] + [from_x(column, d) for d in range(1, X)], axis=0)
-    cut = plane.shape[0] // 2
-    ahead, behind = from_y(plane, 1), from_y(plane, -1)
-    plane_other = from_cfg(plane)
+    all_totals = totals + from_zl(totals)
+    advantage = rewards - jnp.sum(member * all_totals[None, :], axis=1) / GROUP_SIZE
+    rest = after(others, ahead_own, behind_own, totals)
+    ahead, behind = from_y(rest, 1), from_y(rest, -1)
+    early = [from_cfg(piece) for piece in (column, ahead_own, behind_own, far_own)]
     second_part = exchange(
-        after(pack_queries(image_projections, 1), plane_other, first_part)
-    )
-    far_first = from_y(ahead[:cut], 1)
-    far_second = from_y(behind[cut:], -1)
-    own = [plane, ahead, behind, far_first, far_second]
-    pieces = own + [plane_other] + [from_cfg(piece) for piece in own[1:]]
+        after(pack_queries(image_projections, 1), first_part, all_totals, *early, ahead, behind)
+    )
+    far_first = from_y(ahead[:depth], 1)
+    far_second = from_y(behind[depth:], -1)
+    late = [from_cfg(piece) for piece in (others, ahead, behind, far_first, far_second)]
+    pieces = [column, others, ahead_own, ahead, behind_own, behind, far_own, far_first, far_second]
+    pieces += [early[0], late[0], early[1], late[1], early[2], late[2], early[3], late[3], late[4]]
 
     spread = noise_level * jnp.sqrt(timestep / (1.0 - timestep))
     drift_gain = 1.0 + spread * spread * (1.0 - timestep) / (2.0 * timestep)
@@ -414,9 +436,9 @@
     queries_at = per_dev * 2 * kv_rows // image_count
     attended = attention(first_part, queries_at, first_part, 0, image_count, kv_rows, per_dev)
     attended = attention(
-        after(second_part, ahead, behind), 0, first_part, 1, image_count, kv_rows, per_dev, (attended,)
-    )
-    returned = after(exchange(attended), terms)
+        second_part, 0, first_part, 1, image_count, kv_rows, per_dev, (attended,)
+    )
+    returned = after(exchange(after(attended, far_first, far_second)), terms)
     hidden, velocity = hidden_rows(
         place, returned, image_state, modulation[0].transpose(1, 0, 2), final_weight.T, pieces
     )

time: 243 us -> 275 us (1.13)
  starting transfers between devices: 71 us -> 95.8 us
  waiting for transfers between devices: 93.6 us -> 78.9 us
  local copies, waits for them, and re-layouts: 12.1 us -> 21.5 us
  blocking collectives: 11.8 us -> 20.9 us
    all_to_all x3, waiting for transfers between devices: 35.2 us -> 18.6 us  [exchange(): return lax.all_to_all(send, 'seq', split_axis=0, concat_axis=0, tiled=True)]
    ppermute x7 -> x10, waiting for transfers between devices: 17.8 us -> 1.99 us  [from_y(): return lax.ppermute(value, 'dp', pairs)]
    ppermute x1, waiting for transfers between devices: 1.37 us -> 17 us  [from_zl(): return lax.ppermute(value, 'dp', pairs)]
    ppermute x1, starting transfers between devices: 1.4 us -> 12 us  [from_zl(): return lax.ppermute(value, 'dp', pairs)]
    unnamed x32 -> x75, local copies, waits for them, and re-layouts: 8.25 us -> 18.4 us
    all_to_all x1, blocking collectives: 11.8 us -> 20.9 us  [per_device(): lax.all_to_all(kept, 'dp', split_axis=0, concat_axis=0, tiled=True)]
    all_to_all x3, starting transfers between devices: 20 us -> 25.7 us  [exchange(): return lax.all_to_all(send, 'seq', split_axis=0, concat_axis=0, tiled=True)]
    ppermute x8 -> x12, starting transfers between devices: 12.2 us -> 17.2 us  [from_cfg(): return lax.ppermute(value, 'cfg', [(0, 1), (1, 0)])]
  transfers between devices with their start and end apart: 32 -> 39, of which waited for: 20 -> 16; matrix products, arithmetic and copies ran while one was open for 3% -> 2% of each run, Pallas kernels for 6% -> 12%
where the time goes in v1:
time: 275 us; the launch traced here: 272 us
  starting transfers between devices  95.8 us (35%)
  waiting for transfers between devices  78.9 us (29%)
  Pallas kernels  50.9 us (19%)
  local copies, waits for them, and re-layouts  21.5 us (8%)
  blocking collectives  20.9 us (8%)
    pallas_call x2, Pallas kernels, attention(): pl.pallas_call(attention_kernel, grid=(1,), in_specs=[pl.BlockSpec((peers...  31.6 us
    ppermute x6, waiting for transfers between devices, from_x(): return lax.ppermute(value, 'seq', pairs)  28.3 us
    all_to_all x3, starting transfers between devices, exchange(): return lax.all_to_all(send, 'seq', split_axis=0, concat_axis=0, tiled=True)  25.7 us
    all_to_all x1, blocking collectives, per_device(): lax.all_to_all(kept, 'dp', split_axis=0, concat_axis=0, tiled=True)  20.9 us
    all_to_all x3, waiting for transfers between devices, exchange(): return lax.all_to_all(send, 'seq', split_axis=0, concat_axis=0, tiled=True)  18.6 us
    unnamed x75, local copies, waits for them, and re-layouts  18.4 us
    ppermute x12, starting transfers between devices, from_cfg(): return lax.ppermute(value, 'cfg', [(0, 1), (1, 0)])  17.2 us
    ppermute x1, waiting for transfers between devices, from_zl(): return lax.ppermute(value, 'dp', pairs)  17 us
  transfers between devices with their start and end apart: 39, of which 16 were waited for; matrix products, arithmetic and copies ran while one was open for 2% of the time, Pallas kernels for 12%

profile of v1, /device:TPU:1, one launch (start us, length us, event | category | flops | bytes accessed | tf_op | source)
XLA Modules:
  0.0 271.9 jit_solution(7947707613449972898)
XLA Ops:
  0.6 4.4 %pack.1 = bf16[16,768,128]{2,1,0:T(8,128)(2,1)} custom-call(bf16[1,2,128,6144]{3,2,1,0:T(8,128)(2,1)} %q_ref.3, bf16[1,2,128,6144]{3,2,1,0:T(8,128)(2,1)} %q_ref.3, bf16[1,2,32,4096]{3,2,1,0:T(8,128)(2,1)} %vt_ref.1, bf16[1,2,32,4096]{3,2,1,0:T(8,128)(2,1)} %vt_ref.1, bf16[1,2,128,6144]{3,2,1,0:T(8,128)(2,1)} %q_ref.3), custom_call_target="tpu_custom_call" | custom-call | bytes 6291456 | tf_op jit(solution)/shard_map/pack/pallas_call | solution.py:102
  5.0 4.9 %collective-permute-start.4 = (bf16[128,384]{1,0:T(8,128)(2,1)S(1)}, bf16[128,384]{1,0:T(8,128)(2,1)S(1)}, u32[]{:S(2)}, u32[]{:S(2)}) collective-permute-start(bf16[128,384]{1,0:T(8,128)(2,1)S(1)} %copy-done.33), channel_id=1, source_target_pairs={{0,0},{128,1},{2,2},{130,3},{4,4},{132,5},{6,6},{134,7},{8,8},{136... | collective-permute-start | bytes 294920 | tf_op jit(solution)/shard_map/ppermute | solution.py:43
  10.0 2.8 %collective-permute-start.7 = (bf16[128,384]{1,0:T(8,128)(2,1)S(1)}, bf16[128,384]{1,0:T(8,128)(2,1)S(1)}, u32[]{:S(2)}, u32[]{:S(2)}) collective-permute-start(bf16[128,384]{1,0:T(8,128)(2,1)S(1)} %copy-done.33), channel_id=1, source_target_pairs={{24,0},{152,1},{26,2},{154,3},{28,4},{156,5},{30,6},{158,7},{0,8},... | collective-permute-start | bytes 294920 | tf_op jit(solution)/shard_map/ppermute | solution.py:43
  12.8 3.9 %collective-permute-start.6 = (bf16[128,384]{1,0:T(8,128)(2,1)S(1)}, bf16[128,384]{1,0:T(8,128)(2,1)S(1)}, u32[]{:S(2)}, u32[]{:S(2)}) collective-permute-start(bf16[128,384]{1,0:T(8,128)(2,1)S(1)} %copy-done.33), channel_id=1, source_target_pairs={{16,0},{144,1},{18,2},{146,3},{20,4},{148,5},{22,6},{150,7},{24,8}... | collective-permute-start | bytes 294920 | tf_op jit(solution)/shard_map/ppermute | solution.py:43
  16.6 2.5 collective-permute-start.5
  19.2 5.8 %collective-permute-done.5 = bf16[128,384]{1,0:T(8,128)(2,1)S(1)} collective-permute-done((bf16[128,384]{1,0:T(8,128)(2,1)S(1)}, bf16[128,384]{1,0:T(8,128)(2,1)S(1)}, u32[]{:S(2)}, u32[]{:S(2)}) %collective-permute-start.5) | collective-permute-done | bytes 98336 | tf_op jit(solution)/shard_map/ppermute | solution.py:43
  25.1 6.3 %all-to-all-start = ((bf16[16,768,128]{2,1,0:T(8,128)(2,1)}), bf16[16,768,128]{2,1,0:T(8,128)(2,1)}, u32[]{:S(2)}, u32[]{:S(2)}) async-start(bf16[16,768,128]{2,1,0:T(8,128)(2,1)} %pack.1), calls=%async_computation | async-start | bytes 6291456 | tf_op jit(solution)/shard_map/all_to_all | solution.py:369
  31.4 2.5 collective-permute-start.15
  40.1 1.7 collective-permute-done
  43.2 9.2 %collective-permute-done.15 = bf16[512,384]{1,0:T(8,128)(2,1)S(1)} collective-permute-done((bf16[512,384]{1,0:T(8,128)(2,1)S(1)}, bf16[512,384]{1,0:T(8,128)(2,1)S(1)}, u32[]{:S(2)}, u32[]{:S(2)}) %collective-permute-start.15) | collective-permute-done | bytes 393248 | tf_op jit(solution)/shard_map/ppermute | solution.py:28
  52.4 4.1 %collective-permute-done.16 = bf16[512,384]{1,0:T(8,128)(2,1)S(1)} collective-permute-done((bf16[512,384]{1,0:T(8,128)(2,1)S(1)}, bf16[512,384]{1,0:T(8,128)(2,1)S(1)}, u32[]{:S(2)}, u32[]{:S(2)}) %collective-permute-start.16) | collective-permute-done | bytes 393248 | tf_op jit(solution)/shard_map/ppermute | solution.py:28
  56.5 10.5 %collective-permute-done.17 = bf16[512,384]{1,0:T(8,128)(2,1)S(1)} collective-permute-done((bf16[512,384]{1,0:T(8,128)(2,1)S(1)}, bf16[512,384]{1,0:T(8,128)(2,1)S(1)}, u32[]{:S(2)}, u32[]{:S(2)}) %collective-permute-start.17) | collective-permute-done | bytes 393248 | tf_op jit(solution)/shard_map/ppermute | solution.py:28
  72.6 12.0 %collective-permute-start.3 = (f32[8]{0:T(128)S(1)}, f32[8]{0:T(128)S(1)}, u32[]{:S(2)}, u32[]{:S(2)}) collective-permute-start(f32[8]{0:T(128)S(1)} %add_add_fusion.2), channel_id=1, source_target_pairs={{1,0},{0,1},{3,2},{2,3},{5,4},{4,5},{7,6},{6,7},{9,8},{8,9},{11,10... | collective-permute-start | bytes 104 | tf_op jit(solution)/shard_map/ppermute | solution.py:58
  84.6 17.0 %collective-permute-done.3 = f32[8]{0:T(128)S(1)} collective-permute-done((f32[8]{0:T(128)S(1)}, f32[8]{0:T(128)S(1)}, u32[]{:S(2)}, u32[]{:S(2)}) %collective-permute-start.3) | collective-permute-done | bytes 64 | tf_op jit(solution)/shard_map/ppermute | solution.py:58
  103.4 1.8 collective-permute-start.14
  108.5 10.4 %all-to-all-start.1 = ((bf16[16,128,128]{2,1,0:T(8,128)(2,1)}), bf16[16,128,128]{2,1,0:T(8,128)(2,1)S(1)}, u32[]{:S(2)}, u32[]{:S(2)}) async-start(bf16[16,128,128]{2,1,0:T(8,128)(2,1)} %copy-done.1), calls=%async_computation.1 | async-start | bytes 1048576 | tf_op jit(solution)/shard_map/all_to_all | solution.py:369
  121.4 1.8 slice.20
  123.2 2.2 collective-permute-start.20
  125.4 9.2 %attention0.1.rest_0_ = bf16[16,256,128]{2,1,0:T(8,128)(2,1)} custom-call(bf16[16,768,128]{2,1,0:T(8,128)(2,1)} %all-to-all-done.q_ref.kv_ref, bf16[16,768,128]{2,1,0:T(8,128)(2,1)} %all-to-all-done.q_ref.kv_ref), custom_call_target="tpu_custom_call" | custom-call | flops 5368709120 | bytes 2359296 | tf_op jit(solution)/shard_map/attention0/pallas_call | solution.py:162
  135.3 22.4 %attention1.1 = bf16[16,256,128]{2,1,0:T(8,128)(2,1)} custom-call(bf16[16,128,128]{2,1,0:T(8,128)(2,1)} %copy-done.30, bf16[16,768,128]{2,1,0:T(8,128)(2,1)} %all-to-all-done.q_ref.kv_ref, bf16[16,256,128]{2,1,0:T(8,128)(2,1)} %attention0.1.rest_0_), custom_call_target="tpu_custom_call", output_to_operand_aliasing={{}: (2, {})} | custom-call | flops 5368709120 | bytes 2359296 | tf_op jit(solution)/shard_map/attention1/pallas_call | solution.py:162
  158.8 9.1 %all-to-all-start.2 = ((bf16[16,256,128]{2,1,0:T(8,128)(2,1)}), bf16[16,256,128]{2,1,0:T(8,128)(2,1)S(1)}, u32[]{:S(2)}, u32[]{:S(2)}) async-start(bf16[16,256,128]{2,1,0:T(8,128)(2,1)} %attention1.1), calls=%async_computation.2 | async-start | bytes 2097152 | tf_op jit(solution)/shard_map/all_to_all | solution.py:369
  167.9 1.8 collective-permute-start.22
  171.2 18.6 %all-to-all-done.2.heads_ref = bf16[16,256,128]{2,1,0:T(8,128)(2,1)S(1)} async-done(((bf16[16,256,128]{2,1,0:T(8,128)(2,1)}), bf16[16,256,128]{2,1,0:T(8,128)(2,1)S(1)}, u32[]{:S(2)}, u32[]{:S(2)}) %all-to-all-start.2) | async-done | bytes 1048608 | tf_op jit(solution)/shard_map/all_to_all | solution.py:369
  201.0 12.2 %hidden.1 = (bf16[256,3072]{1,0:T(8,128)(2,1)}, f32[64,256]{1,0:T(8,128)S(1)}) custom-call(s32[4]{0:T(128)S(1)} %pad_add_fusion.place, bf16[16,256,128]{2,1,0:T(8,128)(2,1)S(1)} %all-to-all-done.2.heads_ref, bf16[1,2,128,3072]{3,2,1,0:T(8,128)(2,1)} %state_any.1, bf16[3,2,3072]{2,1,0:T(2,128)(2,1)S(1)} %bitcast.21, bf16[64,3072]{1,0:T(8,128)(2,1)S(1)} %bitcast.18, ...), custom_call_target="tpu_custom_call" | custom-call | flops 3221225472 | bytes 12582912 | tf_op jit(solution)/shard_map/hidden/pallas_call | solution.py:264
  213.2 4.3 %collective-permute-start.27 = (f32[64,256]{1,0:T(8,128)S(1)}, f32[64,256]{1,0:T(8,128)S(1)}, u32[]{:S(2)}, u32[]{:S(2)}) collective-permute-start(f32[64,256]{1,0:T(8,128)S(1)} %get-tuple-element.19.own_ref), channel_id=1, source_target_pairs={{0,128},{128,0},{1,129},{129,1},{2,130},{130,2},{3,131},{131,3},{4... | collective-permute-start | bytes 196616 | tf_op jit(solution)/shard_map/ppermute | solution.py:62
  222.7 20.9 %all_to_all.20.parts_ref = f32[8,32,384]{2,1,0:T(8,128)} all-to-all(f32[8,32,384]{2,1,0:T(8,128)S(1)} %add.49), channel_id=1, replica_groups=mesh['cfg'=2,'seq'=16,'dp'=8] {'dp'}, dimensions={0} | all-to-all | bytes 786432 | tf_op jit(solution)/shard_map/all_to_all | solution.py:457
  245.2 3.1 %collective-permute-start.31 = (f32[40,384]{1,0:T(8,128)}, f32[40,384]{1,0:T(8,128)S(1)}, u32[]{:S(2)}, u32[]{:S(2)}) collective-permute-start(f32[40,384]{1,0:T(8,128)} %fold.1), channel_id=1, source_target_pairs={{24,0},{0,8},{8,16},{16,24},{56,32},{32,40},{40,48},{48,56},{88,64... | collective-permute-start | bytes 184328 | tf_op jit(solution)/shard_map/ppermute | solution.py:48
  248.8 2.8 %collective-permute-start.29 = (f32[40,384]{1,0:T(8,128)}, f32[40,384]{1,0:T(8,128)S(1)}, u32[]{:S(2)}, u32[]{:S(2)}) collective-permute-start(f32[40,384]{1,0:T(8,128)} %fold.1), channel_id=1, source_target_pairs={{16,0},{24,8},{0,16},{8,24},{48,32},{56,40},{32,48},{40,56},{80,64... | collective-permute-start | bytes 184328 | tf_op jit(solution)/shard_map/ppermute | solution.py:48
  252.8 3.3 %collective-permute-done.29 = f32[40,384]{1,0:T(8,128)S(1)} collective-permute-done((f32[40,384]{1,0:T(8,128)}, f32[40,384]{1,0:T(8,128)S(1)}, u32[]{:S(2)}, u32[]{:S(2)}) %collective-permute-start.29) | collective-permute-done | bytes 61472 | tf_op jit(solution)/shard_map/ppermute | solution.py:48
  257.1 2.7 collective-permute-start.33
  261.5 2.8 %collective-permute-done.32 = f32[40,384]{1,0:T(8,128)S(1)} collective-permute-done((f32[40,384]{1,0:T(8,128)S(1)}, f32[40,384]{1,0:T(8,128)S(1)}, u32[]{:S(2)}, u32[]{:S(2)}) %collective-permute-start.32) | collective-permute-done | bytes 61472 | tf_op jit(solution)/shard_map/ppermute | solution.py:28
  264.4 5.7 %collective-permute-start.35 = (f32[40,384]{1,0:T(8,128)S(1)}, f32[40,384]{1,0:T(8,128)S(1)}, u32[]{:S(2)}, u32[]{:S(2)}) collective-permute-start(f32[40,384]{1,0:T(8,128)S(1)} %add_add_fusion), channel_id=1, source_target_pairs={{0,128},{128,0},{1,129},{129,1},{2,130},{130,2},{3,131},{131,3},{4... | collective-permute-start | bytes 184328 | tf_op jit(solution)/shard_map/ppermute | solution.py:62
  (149 shorter events, 48.0 us)
Async XLA Ops:
  5.0 14.1 %collective-permute-start.4 = (bf16[128,384]{1,0:T(8,128)(2,1)S(1)}, bf16[128,384]{1,0:T(8,128)(2,1)S(1)}, u32[]{:S(2)}, u32[]{:S(2)}) collective-permute-start(bf16[128,384]{1,0:T(8,128)(2,1)S(1)} %copy-done.33), channel_id=1, source_target_pairs={{0,0},{128,1},{2,2},{130,3},{4,4},{132,5},{6,6},{134,7},{8,8},{136... | collective-permute-start | bytes 294920 | tf_op jit(solution)/shard_map/ppermute | solution.py:43
  10.0 15.1 %collective-permute-start.7 = (bf16[128,384]{1,0:T(8,128)(2,1)S(1)}, bf16[128,384]{1,0:T(8,128)(2,1)S(1)}, u32[]{:S(2)}, u32[]{:S(2)}) collective-permute-start(bf16[128,384]{1,0:T(8,128)(2,1)S(1)} %copy-done.33), channel_id=1, source_target_pairs={{24,0},{152,1},{26,2},{154,3},{28,4},{156,5},{30,6},{158,7},{0,8},... | collective-permute-start | bytes 294920 | tf_op jit(solution)/shard_map/ppermute | solution.py:43
  12.8 12.3 %collective-permute-start.6 = (bf16[128,384]{1,0:T(8,128)(2,1)S(1)}, bf16[128,384]{1,0:T(8,128)(2,1)S(1)}, u32[]{:S(2)}, u32[]{:S(2)}) collective-permute-start(bf16[128,384]{1,0:T(8,128)(2,1)S(1)} %copy-done.33), channel_id=1, source_target_pairs={{16,0},{144,1},{18,2},{146,3},{20,4},{148,5},{22,6},{150,7},{24,8}... | collective-permute-start | bytes 294920 | tf_op jit(solution)/shard_map/ppermute | solution.py:43
  16.6 8.4 %collective-permute-start.5 = (bf16[128,384]{1,0:T(8,128)(2,1)S(1)}, bf16[128,384]{1,0:T(8,128)(2,1)S(1)}, u32[]{:S(2)}, u32[]{:S(2)}) collective-permute-start(bf16[128,384]{1,0:T(8,128)(2,1)S(1)} %copy-done.33), channel_id=1, source_target_pairs={{8,0},{136,1},{10,2},{138,3},{12,4},{140,5},{14,6},{142,7},{16,8},... | collective-permute-start | bytes 294920 | tf_op jit(solution)/shard_map/ppermute | solution.py:43
  25.1 83.4 %all-to-all-start = ((bf16[16,768,128]{2,1,0:T(8,128)(2,1)}), bf16[16,768,128]{2,1,0:T(8,128)(2,1)}, u32[]{:S(2)}, u32[]{:S(2)}) async-start(bf16[16,768,128]{2,1,0:T(8,128)(2,1)} %pack.1), calls=%async_computation | async-start | bytes 6291456 | tf_op jit(solution)/shard_map/all_to_all | solution.py:369
  31.4 20.9 %collective-permute-start.15 = (bf16[512,384]{1,0:T(8,128)(2,1)S(1)}, bf16[512,384]{1,0:T(8,128)(2,1)S(1)}, u32[]{:S(2)}, u32[]{:S(2)}) collective-permute-start(bf16[512,384]{1,0:T(8,128)(2,1)S(1)} %constant_dynamic-update-slice_fusion.rest_0_), channel_id=1, source_target_pairs={{32,0},{40,8},{48,16},{56,24},{64,32},{72,40},{80,48},{88,56},{96,... | collective-permute-start | bytes 1179656 | tf_op jit(solution)/shard_map/ppermute | solution.py:28
  34.0 22.5 %collective-permute-start.16 = (bf16[512,384]{1,0:T(8,128)(2,1)S(1)}, bf16[512,384]{1,0:T(8,128)(2,1)S(1)}, u32[]{:S(2)}, u32[]{:S(2)}) collective-permute-start(bf16[512,384]{1,0:T(8,128)(2,1)S(1)} %constant_dynamic-update-slice_fusion.rest_0_), channel_id=1, source_target_pairs={{64,0},{72,8},{80,16},{88,24},{96,32},{104,40},{112,48},{120,56},{... | collective-permute-start | bytes 1179656 | tf_op jit(solution)/shard_map/ppermute | solution.py:28
  39.1 27.9 %collective-permute-start.17 = (bf16[512,384]{1,0:T(8,128)(2,1)S(1)}, bf16[512,384]{1,0:T(8,128)(2,1)S(1)}, u32[]{:S(2)}, u32[]{:S(2)}) collective-permute-start(bf16[512,384]{1,0:T(8,128)(2,1)S(1)} %constant_dynamic-update-slice_fusion.rest_0_), channel_id=1, source_target_pairs={{96,0},{104,8},{112,16},{120,24},{0,32},{8,40},{16,48},{24,56},{32... | collective-permute-start | bytes 1179656 | tf_op jit(solution)/shard_map/ppermute | solution.py:28
  39.6 27.4 %collective-permute-start.11 = (bf16[512,384]{1,0:T(8,128)(2,1)S(1)}, bf16[512,384]{1,0:T(8,128)(2,1)S(1)}, u32[]{:S(2)}, u32[]{:S(2)}) collective-permute-start(bf16[512,384]{1,0:T(8,128)(2,1)S(1)} %constant_dynamic-update-slice_fusion.rest_0_), channel_id=1, source_target_pairs={{6,0},{7,1},{0,2},{1,3},{2,4},{3,5},{4,6},{5,7},{14,8},{15,9},{8,1... | collective-permute-start | bytes 1179656 | tf_op jit(solution)/shard_map/ppermute | solution.py:53
  41.8 25.3 %collective-permute-start.9 = (bf16[512,384]{1,0:T(8,128)(2,1)S(1)}, bf16[512,384]{1,0:T(8,128)(2,1)S(1)}, u32[]{:S(2)}, u32[]{:S(2)}) collective-permute-start(bf16[512,384]{1,0:T(8,128)(2,1)S(1)} %constant_dynamic-update-slice_fusion.rest_0_), channel_id=1, source_target_pairs={{2,0},{3,1},{4,2},{5,3},{6,4},{7,5},{0,6},{1,7},{10,8},{11,9},{12,... | collective-permute-start | bytes 1179656 | tf_op jit(solution)/shard_map/ppermute | solution.py:53
  67.1 41.4 %collective-permute-start.19 = (bf16[1536,384]{1,0:T(8,128)(2,1)S(1)}, bf16[1536,384]{1,0:T(8,128)(2,1)}, u32[]{:S(2)}, u32[]{:S(2)}) collective-permute-start(bf16[1536,384]{1,0:T(8,128)(2,1)S(1)} %constant_dynamic-update-slice_fusion.4.rest_1_), channel_id=1, source_target_pairs={{6,0},{7,1},{0,2},{1,3},{2,4},{3,5},{4,6},{5,7},{14,8},{15,9},{8,1... | collective-permute-start | bytes 3538952 | tf_op jit(solution)/shard_map/ppermute | solution.py:53
  68.4 40.1 %collective-permute-start.18 = (bf16[1536,384]{1,0:T(8,128)(2,1)S(1)}, bf16[1536,384]{1,0:T(8,128)(2,1)}, u32[]{:S(2)}, u32[]{:S(2)}) collective-permute-start(bf16[1536,384]{1,0:T(8,128)(2,1)S(1)} %constant_dynamic-update-slice_fusion.4.rest_1_), channel_id=1, source_target_pairs={{2,0},{3,1},{4,2},{5,3},{6,4},{7,5},{0,6},{1,7},{10,8},{11,9},{12,... | collective-permute-start | bytes 3538952 | tf_op jit(solution)/shard_map/ppermute | solution.py:53
  69.9 32.5 %collective-permute-start.8 = (bf16[512,384]{1,0:T(8,128)(2,1)S(1)}, bf16[512,384]{1,0:T(8,128)(2,1)S(1)}, u32[]{:S(2)}, u32[]{:S(2)}) collective-permute-start(bf16[512,384]{1,0:T(8,128)(2,1)S(1)} %constant_dynamic-update-slice_fusion.rest_0_), channel_id=1, source_target_pairs={{0,128},{128,0},{1,129},{129,1},{2,130},{130,2},{3,131},{131,3},{4... | collective-permute-start | bytes 1179656 | tf_op jit(solution)/shard_map/ppermute | solution.py:62
  71.2 32.3 %collective-permute-start.13 = (bf16[512,384]{1,0:T(8,128)(2,1)S(1)}, bf16[512,384]{1,0:T(8,128)(2,1)S(1)}, u32[]{:S(2)}, u32[]{:S(2)}) collective-permute-start(bf16[512,384]{1,0:T(8,128)(2,1)S(1)} %collective-permute-done.9.rest_2_), channel_id=1, source_target_pairs={{2,0},{3,1},{4,2},{5,3},{6,4},{7,5},{0,6},{1,7},{10,8},{11,9},{12,... | collective-permute-start | bytes 1179656 | tf_op jit(solution)/shard_map/ppermute | solution.py:53
  72.6 29.1 %collective-permute-start.3 = (f32[8]{0:T(128)S(1)}, f32[8]{0:T(128)S(1)}, u32[]{:S(2)}, u32[]{:S(2)}) collective-permute-start(f32[8]{0:T(128)S(1)} %add_add_fusion.2), channel_id=1, source_target_pairs={{1,0},{0,1},{3,2},{2,3},{5,4},{4,5},{7,6},{6,7},{9,8},{8,9},{11,10... | collective-permute-start | bytes 104 | tf_op jit(solution)/shard_map/ppermute | solution.py:58
  101.7 4.6 %collective-permute-start.12 = (bf16[512,384]{1,0:T(8,128)(2,1)S(1)}, bf16[512,384]{1,0:T(8,128)(2,1)S(1)}, u32[]{:S(2)}, u32[]{:S(2)}) collective-permute-start(bf16[512,384]{1,0:T(8,128)(2,1)S(1)} %collective-permute-done.11.rest_4_), channel_id=1, source_target_pairs={{0,128},{128,0},{1,129},{129,1},{2,130},{130,2},{3,131},{131,3},{4... | collective-permute-start | bytes 1179656 | tf_op jit(solution)/shard_map/ppermute | solution.py:62
  108.5 26.0 %all-to-all-start.1 = ((bf16[16,128,128]{2,1,0:T(8,128)(2,1)}), bf16[16,128,128]{2,1,0:T(8,128)(2,1)S(1)}, u32[]{:S(2)}, u32[]{:S(2)}) async-start(bf16[16,128,128]{2,1,0:T(8,128)(2,1)} %copy-done.1), calls=%async_computation.1 | async-start | bytes 1048576 | tf_op jit(solution)/shard_map/all_to_all | solution.py:369
  120.1 37.7 %collective-permute-start.21 = (bf16[1024,384]{1,0:T(8,128)(2,1)S(1)}, bf16[1024,384]{1,0:T(8,128)(2,1)S(1)}, u32[]{:S(2)}, u32[]{:S(2)}) collective-permute-start(bf16[1024,384]{1,0:T(8,128)(2,1)S(1)} %slice.21), channel_id=1, source_target_pairs={{6,0},{7,1},{0,2},{1,3},{2,4},{3,5},{4,6},{5,7},{14,8},{15,9},{8,1... | collective-permute-start | bytes 2359304 | tf_op jit(solution)/shard_map/ppermute | solution.py:53
  123.2 34.6 %collective-permute-start.20 = (bf16[512,384]{1,0:T(8,128)(2,1)}, bf16[512,384]{1,0:T(8,128)(2,1)S(1)}, u32[]{:S(2)}, u32[]{:S(2)}) collective-permute-start(bf16[512,384]{1,0:T(8,128)(2,1)} %slice.20), channel_id=1, source_target_pairs={{2,0},{3,1},{4,2},{5,3},{6,4},{7,5},{0,6},{1,7},{10,8},{11,9},{12,... | collective-permute-start | bytes 1179656 | tf_op jit(solution)/shard_map/ppermute | solution.py:53
  158.8 31.0 %all-to-all-start.2 = ((bf16[16,256,128]{2,1,0:T(8,128)(2,1)}), bf16[16,256,128]{2,1,0:T(8,128)(2,1)S(1)}, u32[]{:S(2)}, u32[]{:S(2)}) async-start(bf16[16,256,128]{2,1,0:T(8,128)(2,1)} %attention1.1), calls=%async_computation.2 | async-start | bytes 2097152 | tf_op jit(solution)/shard_map/all_to_all | solution.py:369
  167.9 21.9 %collective-permute-start.22 = (bf16[1536,384]{1,0:T(8,128)(2,1)S(1)}, bf16[1536,384]{1,0:T(8,128)(2,1)S(1)}, u32[]{:S(2)}, u32[]{:S(2)}) collective-permute-start(bf16[1536,384]{1,0:T(8,128)(2,1)S(1)} %copy-done.3), channel_id=1, source_target_pairs={{0,128},{128,0},{1,129},{129,1},{2,130},{130,2},{3,131},{131,3},{4... | collective-permute-start | bytes 3538952 | tf_op jit(solution)/shard_map/ppermute | solution.py:62
  169.7 20.2 %collective-permute-start.24 = (bf16[1536,384]{1,0:T(8,128)(2,1)}, bf16[1536,384]{1,0:T(8,128)(2,1)}, u32[]{:S(2)}, u32[]{:S(2)}) collective-permute-start(bf16[1536,384]{1,0:T(8,128)(2,1)} %collective-permute-done.19.rest_5_), channel_id=1, source_target_pairs={{0,128},{128,0},{1,129},{129,1},{2,130},{130,2},{3,131},{131,3},{4... | collective-permute-start | bytes 3538952 | tf_op jit(solution)/shard_map/ppermute | solution.py:62
  169.8 20.1 %collective-permute-start.23 = (bf16[1536,384]{1,0:T(8,128)(2,1)}, bf16[1536,384]{1,0:T(8,128)(2,1)}, u32[]{:S(2)}, u32[]{:S(2)}) collective-permute-start(bf16[1536,384]{1,0:T(8,128)(2,1)} %collective-permute-done.18.rest_3_), channel_id=1, source_target_pairs={{0,128},{128,0},{1,129},{129,1},{2,130},{130,2},{3,131},{131,3},{4... | collective-permute-start | bytes 3538952 | tf_op jit(solution)/shard_map/ppermute | solution.py:62
  170.2 19.6 %collective-permute-start.26 = (bf16[1024,384]{1,0:T(8,128)(2,1)}, bf16[1024,384]{1,0:T(8,128)(2,1)}, u32[]{:S(2)}, u32[]{:S(2)}) collective-permute-start(bf16[1024,384]{1,0:T(8,128)(2,1)} %copy-done.5), channel_id=1, source_target_pairs={{0,128},{128,0},{1,129},{129,1},{2,130},{130,2},{3,131},{131,3},{4... | collective-permute-start | bytes 2359304 | tf_op jit(solution)/shard_map/ppermute | solution.py:62
  170.5 19.3 %collective-permute-start.25 = (bf16[512,384]{1,0:T(8,128)(2,1)}, bf16[512,384]{1,0:T(8,128)(2,1)}, u32[]{:S(2)}, u32[]{:S(2)}) collective-permute-start(bf16[512,384]{1,0:T(8,128)(2,1)} %copy-done.24), channel_id=1, source_target_pairs={{0,128},{128,0},{1,129},{129,1},{2,130},{130,2},{3,131},{131,3},{4... | collective-permute-start | bytes 1179656 | tf_op jit(solution)/shard_map/ppermute | solution.py:62
  213.2 5.2 %collective-permute-start.27 = (f32[64,256]{1,0:T(8,128)S(1)}, f32[64,256]{1,0:T(8,128)S(1)}, u32[]{:S(2)}, u32[]{:S(2)}) collective-permute-start(f32[64,256]{1,0:T(8,128)S(1)} %get-tuple-element.19.own_ref), channel_id=1, source_target_pairs={{0,128},{128,0},{1,129},{129,1},{2,130},{130,2},{3,131},{131,3},{4... | collective-permute-start | bytes 196616 | tf_op jit(solution)/shard_map/ppermute | solution.py:62
  245.2 6.4 %collective-permute-start.31 = (f32[40,384]{1,0:T(8,128)}, f32[40,384]{1,0:T(8,128)S(1)}, u32[]{:S(2)}, u32[]{:S(2)}) collective-permute-start(f32[40,384]{1,0:T(8,128)} %fold.1), channel_id=1, source_target_pairs={{24,0},{0,8},{8,16},{16,24},{56,32},{32,40},{40,48},{48,56},{88,64... | collective-permute-start | bytes 184328 | tf_op jit(solution)/shard_map/ppermute | solution.py:48
  248.3 4.5 %collective-permute-start.30 = (f32[40,384]{1,0:T(8,128)}, f32[40,384]{1,0:T(8,128)S(1)}, u32[]{:S(2)}, u32[]{:S(2)}) collective-permute-start(f32[40,384]{1,0:T(8,128)} %fold.1), channel_id=1, source_target_pairs={{8,0},{16,8},{24,16},{0,24},{40,32},{48,40},{56,48},{32,56},{72,64... | collective-permute-start | bytes 184328 | tf_op jit(solution)/shard_map/ppermute | solution.py:48
  248.8 7.3 %collective-permute-start.29 = (f32[40,384]{1,0:T(8,128)}, f32[40,384]{1,0:T(8,128)S(1)}, u32[]{:S(2)}, u32[]{:S(2)}) collective-permute-start(f32[40,384]{1,0:T(8,128)} %fold.1), channel_id=1, source_target_pairs={{16,0},{24,8},{0,16},{8,24},{48,32},{56,40},{32,48},{40,56},{80,64... | collective-permute-start | bytes 184328 | tf_op jit(solution)/shard_map/ppermute | solution.py:48
  257.1 4.5 %collective-permute-start.33 = (f32[40,384]{1,0:T(8,128)S(1)}, f32[40,384]{1,0:T(8,128)S(1)}, u32[]{:S(2)}, u32[]{:S(2)}) collective-permute-start(f32[40,384]{1,0:T(8,128)S(1)} %add_add_fusion.1), channel_id=1, source_target_pairs={{32,0},{40,8},{48,16},{56,24},{64,32},{72,40},{80,48},{88,56},{96,... | collective-permute-start | bytes 184328 | tf_op jit(solution)/shard_map/ppermute | solution.py:28
  259.7 4.6 %collective-permute-start.32 = (f32[40,384]{1,0:T(8,128)S(1)}, f32[40,384]{1,0:T(8,128)S(1)}, u32[]{:S(2)}, u32[]{:S(2)}) collective-permute-start(f32[40,384]{1,0:T(8,128)S(1)} %add_add_fusion.1), channel_id=1, source_target_pairs={{64,0},{72,8},{80,16},{88,24},{96,32},{104,40},{112,48},{120,56},{... | collective-permute-start | bytes 184328 | tf_op jit(solution)/shard_map/ppermute | solution.py:28
  264.4 6.6 %collective-permute-start.35 = (f32[40,384]{1,0:T(8,128)S(1)}, f32[40,384]{1,0:T(8,128)S(1)}, u32[]{:S(2)}, u32[]{:S(2)}) collective-permute-start(f32[40,384]{1,0:T(8,128)S(1)} %add_add_fusion), channel_id=1, source_target_pairs={{0,128},{128,0},{1,129},{129,1},{2,130},{130,2},{3,131},{131,3},{4... | collective-permute-start | bytes 184328 | tf_op jit(solution)/shard_map/ppermute | solution.py:62
  (42 other events, 402.3 us)
